TPU v7x, 32 devices: a whole 2x2x4 slice. The times are simulated.
32 devices in a mesh: groups: 2 (over x), eigen: 16 (over z, y, core).
Axes of the slice: x: 2, y: 2, z: 4, core: 2. Of those that a mesh axis runs over, the one named last changes fastest.
Arguments:
- acts: bfloat16 [64, 8192], P(('groups', 'eigen')), parts along dimension 0, may hold values from -6 to 6
- grads: bfloat16 [64, 8192], P(('groups', 'eigen')), parts along dimension 0, may hold values from -0.75 to 0.75
- lengths: int32 [8], P('groups'), parts along dimension 0, may hold values from 1 to 16, 32 in all
- basis_in: float32 [16384, 8192], P('groups', 'eigen'), parts along dimension 0
- basis_out: float32 [16384, 8192], P('groups', 'eigen'), parts along dimension 0
Outputs:
- corrections: float32 [16384, 8192], P('groups', 'eigen'), parts along dimension 0
- precond: float32 [256, 8192], P('groups', 'eigen'), parts along dimension 0
There are 2 independent parts, one for each index of `groups`. A program takes and returns all parts, laid end to end along the dimension named above; each array names one. Nothing has to cross between parts.
Inputs may be any that keep to these rules, and one draw needn't show every extreme that they name: The lengths sum to 32; the longest is exactly 16.
All inputs are finite; a program needn't handle non-finite values.
Results may differ from a plain program's by a relative error of at most 0.0066.
Values may be sent and summed in bfloat16 or wider, within the bound.
A program may use at most 192 MiB of HBM per device.

v0:
```python
import jax
import jax.numpy as jnp
from jax import lax
from jax.sharding import PartitionSpec as P

SEQS = 4
OUT_ROWS = 128


damp_share = 0.1


def rotate(rows, basis):
    product = jnp.dot(
        rows.astype(jnp.float32),
        basis,
        precision=lax.Precision.HIGHEST,
        preferred_element_type=jnp.float32,
    )
    return product.astype(jnp.bfloat16)


def per_device(acts, grads, lengths, basis_in, basis_out):
    highest = lax.Precision.HIGHEST
    whole_acts, whole_grads = (
        lax.all_gather(acts, "eigen", axis=0, tiled=True),
        lax.all_gather(grads, "eigen", axis=0, tiled=True),
    )
    rot_out = rotate(whole_grads, basis_out)
    rot_in = rotate(whole_acts, basis_in)
    token_count = rot_in.shape[0]
    span = token_count // 2
    ends = jnp.cumsum(lengths)
    starts = ends - lengths
    clamped = jnp.minimum(starts, token_count - span)
    offsets = jnp.arange(span, dtype=jnp.int32)
    window_list = []
    for seq_id in range(SEQS):
        where = clamped[seq_id] + offsets
        inside = ((where >= starts[seq_id]) & (where < ends[seq_id])).astype(jnp.bfloat16)
        rows_in = lax.dynamic_slice_in_dim(rot_in, clamped[seq_id], span, 0)
        window_list.append(rows_in * inside[:, None])
    masked_windows = jnp.stack(window_list, 0)
    piece = lax.all_gather(rot_out, "eigen", axis=1, tiled=True)
    pieces = jnp.stack(
        [lax.dynamic_slice_in_dim(piece, clamped[seq_id], span, 0) for seq_id in range(SEQS)], 0
    )
    product = jnp.einsum("swc,swd->scd", pieces, masked_windows, preferred_element_type=jnp.float32)
    total = jnp.sum(product, 0)
    squares = jnp.sum(product * product, 0)
    stacked = jnp.stack([squares / SEQS, total / SEQS], 0)
    corrections = stacked[0]
    mean_rot = stacked[1]
    total_all = lax.psum(jnp.sum(corrections), "eigen")
    entries = corrections.shape[0] * basis_in.shape[0]
    damping = damp_share * (total_all / entries)
    scaled = mean_rot / (corrections + damping)
    window = basis_out[:OUT_ROWS, :]
    left_part = jnp.dot(
        lax.all_gather(window, "eigen", axis=1, tiled=True),
        scaled,
        precision=highest,
        preferred_element_type=jnp.float32,
    )
    own_rows = lax.psum_scatter(
        jnp.dot(basis_in, left_part.T, precision=highest, preferred_element_type=jnp.float32),
        "eigen",
        scatter_dimension=0,
        tiled=True,
    )
    precond = own_rows.T
    return (corrections, precond)


def solution(mesh):
    in_specs = (
        P(("groups", "eigen"), None),
        P(("groups", "eigen"), None),
        P("groups"),
        P("groups", "eigen"),
        P("groups", "eigen"),
    )
    out_specs = (P("groups", "eigen"), P("groups", "eigen"))
    return jax.shard_map(
        per_device, mesh=mesh, in_specs=in_specs, out_specs=out_specs, check_vma=False
    )
```

profile of v0, /device:TPU:0, one launch (start us, length us, event | category | flops | bytes accessed | tf_op | source)
XLA Modules:
  0.0 317.7 jit_solution(1676285622429466513)
XLA Ops:
  7.2 0.0 all-gather.4.cloned.1.call-start
  7.2 1.7 slice.63
  8.9 0.0 all-gather.4.cloned.1.call-update
  8.9 0.0 reduce-scatter.2.cloned.1.call-start
  9.0 0.8 reduce-window.4
  9.8 0.7 broadcast_minimum_fusion
  10.4 0.7 fusion.22
  16.1 26.3 %all-gather = bf16[16,2,8192]{2,1,0:T(2,128)(2,1)S(1)} all-gather(bf16[1,2,8192]{2,1,0:T(2,128)(2,1)} %bitcast.44), channel_id=1, replica_groups=mesh['groups'=2,'eigen'=16] {'eigen'}, dimensions={0}, use_global_device_ids=true | all-gather | bytes 557056 | tf_op jit(solution)/shard_map/all_gather | solution.py:27
  42.4 0.2 reshape.53
  42.6 21.0 %all-gather.1 = bf16[16,2,8192]{2,1,0:T(2,128)(2,1)S(1)} all-gather(bf16[1,2,8192]{2,1,0:T(2,128)(2,1)} %bitcast.45), channel_id=1, replica_groups=mesh['groups'=2,'eigen'=16] {'eigen'}, dimensions={0}, use_global_device_ids=true | all-gather | bytes 557056 | tf_op jit(solution)/shard_map/all_gather | solution.py:26
  63.7 0.2 reshape.55
  66.3 0.0 copy-start
  66.4 0.7 fusion.23
  67.0 2.8 and_convert_fusion
  69.8 2.4 and_convert_fusion.1
  72.2 1.8 and_convert_fusion.2
  74.0 2.0 and_convert_fusion.3
  76.0 9.6 %convolution_convert_fusion = bf16[32,512]{1,0:T(8,128)(2,1)S(1)} fusion(bf16[32,8192]{1,0:T(8,128)(2,1)S(1)} %reshape.55, f32[8192,512]{1,0:T(8,128)} %param.8), kind=kOutput, calls=%fused_computation.7 | convolution fusion | flops 1610629120 | bytes 17334272 | tf_op jit(solution)/shard_map/dot_general | solution.py:14
  85.6 0.1 multiply_bitcast_fusion.3
  85.7 0.0 copy-done
  85.7 6.1 %convolution_convert_fusion.1 = bf16[32,512]{1,0:T(8,128)(2,1)S(1)} fusion(bf16[32,8192]{1,0:T(8,128)(2,1)S(1)} %reshape.53, f32[8192,512]{1,0:T(8,128)S(1)} %copy-done), kind=kOutput, calls=%fused_computation.8 | convolution fusion | flops 1610629120 | bytes 17334272 | tf_op jit(solution)/shard_map/dot_general | solution.py:14
  91.9 20.1 %all_gather.13 = bf16[32,8192]{1,0:T(8,128)(2,1)S(1)} all-gather(bf16[32,512]{1,0:T(8,128)(2,1)S(1)} %convolution_convert_fusion.1), channel_id=1, replica_groups=mesh['groups'=2,'eigen'=16] {'eigen'}, dimensions={1}, use_global_device_ids=true | all-gather | bytes 557056 | tf_op jit(solution)/shard_map/all_gather | solution.py:44
  112.0 0.3 dynamic-slice_bitcast_fusion.3
  112.3 26.8 %fusion.20 = (f32[8192,512]{1,0:T(8,128)}, f32[8192,512]{1,0:T(8,128)}) fusion(bf16[1,16,512]{2,1,0:T(8,128)(2,1)S(1)} %get-tuple-element.13, bf16[1,16,512]{2,1,0:T(8,128)(2,1)S(1)} %get-tuple-element.14, bf16[1,16,512]{2,1,0:T(8,128)(2,1)S(1)} %get-tuple-element.15, bf16[1,16,512]{2,1,0:T(8,128)(2,1)S(1)} %get-tuple-element.12, ...), kind=kOutput, calls=%fused_computation.40 | convolution fusion | flops 580485120 | bytes 34668544 | tf_op jit(solution)/shard_map/swc,swd->scd/dot_general | solution.py:48
  139.1 13.5 %fusion.21 = (f32[]{:T(128)}, f32[8192,512]{1,0:T(8,128)}) fusion(f32[8192,512]{1,0:T(8,128)} %get-tuple-element.3), kind=kLoop, calls=%fused_computation.41 | loop fusion | flops 8388607 | bytes 33554436 | tf_op jit(solution)/shard_map/reduce_sum | solution.py:54
  152.6 30.9 %psum.7 = f32[]{:T(128)} all-reduce(f32[]{:T(128)} %get-tuple-element.4), channel_id=1, replica_groups=mesh['groups'=2,'eigen'=16] {'eigen'}, use_global_device_ids=true, to_apply=%region_4.5 | all-reduce | flops 1 | bytes 8 | tf_op jit(solution)/shard_map/psum | solution.py:54
  184.1 0.0 all-gather.4.cloned.1.call-done
  184.1 33.2 %fusion = f32[512,128]{1,0:T(8,128)S(1)} fusion(f32[128,8192]{1,0:T(8,128)} %all-gather.4.cloned.1.call-done, f32[8192,512]{1,0:T(8,128)} %get-tuple-element.5, f32[8192,512]{1,0:T(8,128)} %get-tuple-element.2, f32[]{:T(128)S(6)} %mul_shard_map.3), kind=kOutput, calls=%fused_computation.2 | convolution fusion | flops 6455033856 | bytes 38010884 | tf_op jit(solution)/shard_map/dot_general | solution.py:59
  217.3 24.3 %convolution_bitcast_fusion = f32[8192,128]{0,1:T(8,128)} fusion(f32[512,128]{1,0:T(8,128)S(1)} %fusion, f32[8192,512]{1,0:T(8,128)} %param.8), kind=kOutput, calls=%fused_computation.3 | convolution fusion | flops 6442450944 | bytes 21233664 | tf_op jit(solution)/shard_map/dot_general | solution.py:66
  241.6 0.0 reduce-scatter.2.cloned.1.call-update
  241.6 69.2 %reduce-scatter.2.cloned.1.call-done = f32[512,128]{0,1:T(8,128)} async-done(((f32[8192,128]{0,1:T(8,128)}), f32[512,128]{0,1:T(8,128)}) %reduce-scatter.2.cloned.1.call-update) | async-done | bytes 262160 | tf_op jit(solution)/shard_map/reduce_scatter | solution.py:65
Async XLA Ops:
  7.2 176.9 %all-gather.4.cloned.1.call-start = ((), (), s32[]{:S(2)}) async-start(), calls=%async_computation.1 | async-start | bytes 4456448 | tf_op jit(solution)/shard_map/all_gather | solution.py:60
  8.9 302.0 %reduce-scatter.2.cloned.1.call-start = ((), (), s32[]{:S(2)}) async-start(), calls=%async_computation.2 | async-start | bytes 4456448 | tf_op jit(solution)/shard_map/reduce_scatter | solution.py:65
  66.3 19.4 %copy-start = (f32[8192,512]{1,0:T(8,128)S(1)}, f32[8192,512]{1,0:T(8,128)}, u32[]{:S(2)}) copy-start(f32[8192,512]{1,0:T(8,128)} %param.9) | copy-start | bytes 50331652
Sparse Core Ops, SparseCore 0:
  10.8 59.2 all-gather.3
  241.7 69.0 reduce-scatter.1
where the time goes:
time: 318 us
  matrix products  100 us (31%)
  blocking collectives  98.4 us (31%)
  waiting for transfers between devices  69.3 us (22%)
  other arithmetic  24 us (8%)
  between operations  22.2 us (7%)
  local copies, waits for them, and re-layouts  3.67 us (1%)
    reduce_scatter x1, waiting for transfers between devices, per_device(): lax.psum_scatter(jnp.dot(basis_in, left_part.T, precision=highest, prefer...  69.2 us
    dot_general x1, matrix products, per_device(): jnp.dot(lax.all_gather(window, 'eigen', axis=1, tiled=True), scaled, prec...  33.2 us
    psum x1, blocking collectives, per_device(): total_all = lax.psum(jnp.sum(corrections), 'eigen')  30.9 us
    dot_general x1, matrix products, per_device(): jnp.einsum('swc,swd->scd', pieces, masked_windows, preferred_element_type...  26.8 us
    all_gather x1, blocking collectives, per_device(): lax.all_gather(grads, 'eigen', axis=0, tiled=True)  26.3 us
    dot_general x1, matrix products, per_device(): jnp.dot(basis_in, left_part.T, precision=highest, preferred_element_type=...  24.3 us
    all_gather x1, blocking collectives, per_device(): lax.all_gather(acts, 'eigen', axis=0, tiled=True)  21 us
    all_gather x1, blocking collectives, per_device(): piece = lax.all_gather(rot_out, 'eigen', axis=1, tiled=True)  20.1 us
  transfers between devices with their start and end apart: 2, of which 1 were waited for; matrix products, arithmetic and copies ran while one was open for 22% of the time, Pallas kernels for 0%

commit v1 on v0

v1 whole, which is shorter than its diff:
```python
import functools

import jax
import jax.numpy as jnp
from jax import lax
from jax.experimental import pallas as pl
from jax.experimental.pallas import tpu as pltpu
from jax.sharding import PartitionSpec as P

SEQS = 4
OUT_ROWS = 128
CORES = 2
ROW_TILE = 16
damp_share = 0.1
BF16 = jnp.bfloat16
F32 = jnp.float32
VMEM_BYTES = 56 * 1024 * 1024


def grid_of(n):
    wide = 2 if n <= 16 else 1
    return n // (CORES * wide), wide


class Place:
    def __init__(self, n):
        self.n = n
        self.depth, self.wide = grid_of(n)
        self.me = lax.axis_index("eigen")
        self.core = lax.rem(self.me, CORES)
        self.y = lax.rem(self.me // CORES, self.wide)
        self.z = self.me // (CORES * self.wide)

    def at(self, z, y, core):
        return (z * self.wide + y) * CORES + core


def entry_barrier(place):
    barrier = pltpu.get_barrier_semaphore()
    for step in range(1, place.n):
        other = lax.rem(place.me + step, place.n)
        pl.semaphore_signal(
            barrier, inc=1, device_id={"eigen": other}, device_id_type=pl.DeviceIdType.MESH
        )
    pl.semaphore_wait(barrier, place.n - 1)


def remote(src, dst, send_sem, recv_sem, to):
    return pltpu.make_async_remote_copy(
        src_ref=src,
        dst_ref=dst,
        send_sem=send_sem,
        recv_sem=recv_sem,
        device_id={"eigen": to},
        device_id_type=pl.DeviceIdType.MESH,
    )


class Gather:
    def __init__(self, place, slots, send_sems, recv_sems):
        self.p, self.slots = place, slots
        self.send_sems, self.recv_sems = send_sems, recv_sems

    def copy(self, slot, way, to):
        return remote(
            self.slots.at[slot],
            self.slots.at[slot],
            self.send_sems.at[way, slot],
            self.recv_sems.at[slot],
            to,
        )

    def arrived(self, slot):
        self.copy(slot, 0, self.p.me).wait_recv()

    def up(self, slot, act):
        p = self.p

        @pl.when(p.z < p.depth - 1)
        def _():
            act(self.copy(slot, 0, p.at(p.z + 1, p.y, p.core)))

    def down(self, slot, act):
        p = self.p

        @pl.when(p.z > 0)
        def _():
            act(self.copy(slot, 1, p.at(p.z - 1, p.y, p.core)))

    def across(self, slot, act):
        p = self.p
        if p.wide > 1:
            act(self.copy(slot, 2, p.at(p.z, 1 - p.y, p.core)))
        self.over(slot, act)

    def over(self, slot, act):
        p = self.p
        act(self.copy(slot, 3, p.at(p.z, p.y, 1 - p.core)))

    def beside(self, dz):
        p = self.p
        if p.wide > 1:
            slot = p.at(p.z + dz, 1 - p.y, p.core)
            self.arrived(slot)
            self.over(slot, start)

    def round(self, h):
        p = self.p
        if h == 0:
            self.up(p.me, start)
            self.down(p.me, start)
            self.across(p.me, start)
            return

        @pl.when(p.z - h >= 0)
        def _():
            slot = p.at(p.z - h, p.y, p.core)
            self.arrived(slot)
            self.up(slot, start)
            self.across(slot, start)

        @pl.when(p.z + h < p.depth)
        def _():
            slot = p.at(p.z + h, p.y, p.core)
            self.arrived(slot)
            self.down(slot, start)
            self.across(slot, start)

        self.beside_round(h - 1)

    def beside_round(self, h):
        p = self.p
        if h == 0:
            self.beside(0)
            return

        @pl.when(p.z - h >= 0)
        def _():
            self.beside(-h)

        @pl.when(p.z + h < p.depth)
        def _():
            self.beside(h)

    def last(self):
        p = self.p
        self.beside_round(p.depth - 1)
        for z in range(p.depth):
            for y in range(p.wide):
                self.arrived(p.at(z, y, 1 - p.core))

    def drain(self):
        p = self.p
        for z in range(p.depth):
            slot = p.at(z, p.y, p.core)

            @pl.when(z <= p.z)
            def _():
                self.up(slot, wait_send)

            @pl.when(z >= p.z)
            def _():
                self.down(slot, wait_send)

            self.across(slot, wait_send)
            if p.wide > 1:
                self.over(p.at(z, 1 - p.y, p.core), wait_send)


def start(copy):
    copy.start()


def wait_send(copy):
    copy.wait_send()


def sequence_ends(lengths):
    ends, total = [], 0
    for s in range(SEQS):
        total = total + lengths[s]
        ends.append(total)
    return ends


def sequence_of(position, ends):
    which = jnp.zeros(position.shape, jnp.int32)
    for s in range(SEQS - 1):
        which = which + (position >= ends[s]).astype(jnp.int32)
    return which


def rotate_kernel(
    n,
    rows_ref,
    lengths,
    basis_in,
    basis_out,
    rot_out_hbm,
    window_hbm,
    rot_in_ref,
    damp_ref,
    held,
    tokens,
    window_f32,
    window,
    rot_out,
    parts,
    acc,
    held_sems,
    token_send,
    token_recv,
    window_send,
    window_recv,
    rot_send,
    rot_recv,
    part_send,
    part_recv,
    local_sems,
):
    place = Place(n)
    features, width = basis_in.shape
    steps = held.shape[1]
    chunk = features // steps
    count = rot_in_ref.shape[0]

    def load(which, k):
        source = basis_out if which == 0 else basis_in
        return pltpu.make_async_copy(
            source.at[pl.ds(k * chunk, chunk)], held.at[which, k], held_sems.at[which, k]
        )

    first_rows = pltpu.make_async_copy(
        basis_out.at[pl.ds(0, OUT_ROWS)], window_f32, local_sems.at[0]
    )
    first_rows.start()
    for which in range(2):
        for k in range(steps):
            load(which, k).start()

    tokens[place.me] = rows_ref[...]
    entry_barrier(place)
    token_gather = Gather(place, tokens, token_send, token_recv)
    window_gather = Gather(place, window, window_send, window_recv)
    rot_gather = Gather(place, rot_out, rot_send, rot_recv)
    for h in range(place.depth):
        token_gather.round(h)
    token_gather.last()
    first_rows.wait()
    window[place.me] = window_f32[...].astype(BF16)
    window_gather.round(0)

    def rotate(which, low, high):
        row = lax.broadcasted_iota(jnp.int32, (count, n * ROW_TILE), 0)
        col = lax.broadcasted_iota(jnp.int32, (count, n * ROW_TILE), 1)
        here = pl.ds((1 - which) * ROW_TILE, ROW_TILE)
        flat = tokens[:, here, :].reshape(n * ROW_TILE, chunk)

        def body(k, carry):
            load(which, k).wait()
            pick = (col == row * steps + k).astype(F32).astype(BF16)
            left = jnp.dot(pick, flat, preferred_element_type=F32).astype(BF16)
            block = held[which, k]
            high_part = block.astype(BF16)
            low_part = (block - high_part.astype(F32)).astype(BF16)
            acc[...] += jnp.dot(left, high_part, preferred_element_type=F32) + jnp.dot(
                left, low_part, preferred_element_type=F32
            )
            return carry

        lax.fori_loop(low, high, body, 0)

    half = steps // 2
    rounds = list(range(1, place.depth))
    acc[...] = jnp.zeros_like(acc)
    rotate(0, 0, half)
    for h in rounds[:1]:
        window_gather.round(h)
    rotate(0, half, steps)
    rot_out[place.me] = acc[...].astype(BF16)
    rot_gather.round(0)
    for h in rounds[1:2]:
        window_gather.round(h)
    acc[...] = jnp.zeros_like(acc)
    rotate(1, 0, half)
    for h in rounds[:1]:
        rot_gather.round(h)
    for h in rounds[2:]:
        window_gather.round(h)
    rotate(1, half, steps)
    rot_in = acc[...].astype(BF16)
    rot_in_ref[...] = rot_in
    for h in rounds[1:]:
        rot_gather.round(h)
    rot_gather.last()

    contract = (((1,), (1,)), ((), ()))
    gram_in = lax.dot_general(rot_in, rot_in, contract, preferred_element_type=F32)
    gram_out = jnp.zeros((count, count), F32)
    for d in range(n):
        gram_out += lax.dot_general(rot_out[d], rot_out[d], contract, preferred_element_type=F32)
    ends = sequence_ends(lengths)
    one = sequence_of(lax.broadcasted_iota(jnp.int32, (count, count), 0), ends)
    two = sequence_of(lax.broadcasted_iota(jnp.int32, (count, count), 1), ends)
    inner = jnp.sum(jnp.where(one == two, gram_in * gram_out, 0.0))
    parts[place.me] = jnp.full(parts.shape[1:], inner, F32)

    def part_copy(step):
        other = lax.rem(place.me + step, n)
        return remote(
            parts.at[place.me],
            parts.at[place.me],
            part_send.at[step],
            part_recv.at[place.me],
            other,
        )

    for step in range(1, n):
        part_copy(step).start()
    out_copy = pltpu.make_async_copy(rot_out, rot_out_hbm, local_sems.at[1])
    out_copy.start()
    window_gather.last()
    window_copy = pltpu.make_async_copy(window, window_hbm, local_sems.at[2])
    window_copy.start()
    for step in range(1, n):
        other = lax.rem(place.me + step, n)
        remote(
            parts.at[other], parts.at[other], part_send.at[step], part_recv.at[other], other
        ).wait_recv()
    total = jnp.sum(parts[...], axis=0)
    damp_ref[...] = total * (damp_share / (SEQS * features * (n * width)))
    for step in range(1, n):
        part_copy(step).wait_send()
    token_gather.drain()
    window_gather.drain()
    rot_gather.drain()
    out_copy.wait()
    window_copy.wait()


def rotate_all(n, rows, lengths, basis_in, basis_out):
    features, width = basis_in.shape
    chunk = rows.shape[1]
    steps = features // chunk
    count = n * ROW_TILE // steps
    sems = pltpu.SemaphoreType.DMA
    return pl.pallas_call(
        functools.partial(rotate_kernel, n),
        out_shape=(
            jax.ShapeDtypeStruct((n, count, width), BF16),
            jax.ShapeDtypeStruct((n, OUT_ROWS, width), BF16),
            jax.ShapeDtypeStruct((count, width), BF16),
            jax.ShapeDtypeStruct((8, 128), F32),
        ),
        in_specs=[
            pl.BlockSpec(memory_space=pltpu.VMEM),
            pl.BlockSpec(memory_space=pltpu.SMEM),
            pl.BlockSpec(memory_space=pl.ANY),
            pl.BlockSpec(memory_space=pl.ANY),
        ],
        out_specs=(
            pl.BlockSpec(memory_space=pl.ANY),
            pl.BlockSpec(memory_space=pl.ANY),
            pl.BlockSpec(memory_space=pltpu.VMEM),
            pl.BlockSpec(memory_space=pltpu.VMEM),
        ),
        scratch_shapes=[
            pltpu.VMEM((2, steps, chunk, width), F32),
            pltpu.VMEM((n, 2 * ROW_TILE, chunk), BF16),
            pltpu.VMEM((OUT_ROWS, width), F32),
            pltpu.VMEM((n, OUT_ROWS, width), BF16),
            pltpu.VMEM((n, count, width), BF16),
            pltpu.VMEM((n, 8, 128), F32),
            pltpu.VMEM((count, width), F32),
            sems((2, steps)),
            sems((4, n)),
            sems((n,)),
            sems((4, n)),
            sems((n,)),
            sems((4, n)),
            sems((n,)),
            sems((n,)),
            sems((n,)),
            sems((3,)),
        ],
        compiler_params=pltpu.CompilerParams(
            collective_id=0, has_side_effects=True, vmem_limit_bytes=VMEM_BYTES
        ),
        name="rotate_and_gather",
    )(rows, lengths, basis_in, basis_out)


def correct_kernel(lengths, rot_out, window, rot_in, damp, corrections, left, masked):
    block = pl.program_id(0)
    count, width = rot_in.shape

    @pl.when(block == 0)
    def _():
        which = sequence_of(
            lax.broadcasted_iota(jnp.int32, (count, width), 0), sequence_ends(lengths)
        )
        half = rot_in[...].astype(F32) * 0.5
        for s in range(SEQS):
            masked[:, s * width : (s + 1) * width] = jnp.where(which == s, half, 0.0).astype(BF16)
        left[...] = jnp.zeros_like(left)

    columns = rot_out[0].astype(F32).T.astype(BF16)
    tile = 64
    damping = damp[0:1, 0:1]
    scaled = []
    for low in range(0, columns.shape[0], tile):
        rows = columns[low : low + tile]
        squares, total = None, None
        for s in range(SEQS):
            product = jnp.dot(
                rows, masked[:, s * width : (s + 1) * width], preferred_element_type=F32
            )
            squares = product * product if s == 0 else squares + product * product
            total = product if s == 0 else total + product
        corrections[low : low + tile, :] = squares
        scaled.append((total / (squares + damping)).astype(BF16))
    left[...] += jnp.dot(window[0], jnp.concatenate(scaled, 0), preferred_element_type=F32)

    @pl.when(block == pl.num_programs(0) - 1)
    def _():
        left[...] = left[...] * 0.5


def correct(lengths, rot_out, window, rot_in, damp):
    n, count, width = rot_out.shape
    whole = lambda i: (0, 0)
    return pl.pallas_call(
        correct_kernel,
        grid=(n,),
        out_shape=(
            jax.ShapeDtypeStruct((n * width, width), F32),
            jax.ShapeDtypeStruct((OUT_ROWS, width), F32),
        ),
        in_specs=[
            pl.BlockSpec(memory_space=pltpu.SMEM),
            pl.BlockSpec((1, count, width), lambda i: (i, 0, 0)),
            pl.BlockSpec((1, OUT_ROWS, width), lambda i: (i, 0, 0)),
            pl.BlockSpec((count, width), whole),
            pl.BlockSpec((8, 128), whole),
        ],
        out_specs=(
            pl.BlockSpec((width, width), lambda i: (i, 0)),
            pl.BlockSpec((OUT_ROWS, width), whole),
        ),
        scratch_shapes=[pltpu.VMEM((count, SEQS * width), BF16)],
        compiler_params=pltpu.CompilerParams(vmem_limit_bytes=VMEM_BYTES),
        name="corrections",
    )(lengths, rot_out, window, rot_in, damp)


def back_kernel(
    n,
    left_ref,
    basis,
    out,
    held,
    own,
    core_out,
    core_in,
    y_out,
    y_in,
    z_out,
    from_below,
    from_above,
    held_sems,
    core_send,
    core_recv,
    y_send,
    y_recv,
    z_send,
    below_recv,
    above_recv,
):
    place = Place(n)
    p = place
    width = basis.shape[1]

    def load(d):
        return pltpu.make_async_copy(
            basis.at[pl.ds(pl.multiple_of(d * width, width), width)], held.at[d], held_sems.at[d]
        )

    def in_order(visit):
        for h in range(p.depth - 1, 0, -1):
            for there in (p.z + h, p.z - h):

                @pl.when((there >= 0) & (there < p.depth))
                def _():
                    visit(there)

        visit(p.z)

    def load_all(z):
        for y in range(p.wide):
            for core in range(CORES):
                load(p.at(z, y, core)).start()

    in_order(load_all)
    left = left_ref[...].astype(BF16)
    entry_barrier(place)

    def partial_of(z, y, core):
        d = p.at(z, y, core)
        load(d).wait()
        return lax.dot_general(
            left, held[d].astype(BF16), (((1,), (1,)), ((), ())), preferred_element_type=F32
        )

    sides = [1, 0] if p.wide > 1 else [0]

    def core_copy(z, side):
        k = z * p.wide + side
        return remote(
            core_out.at[k],
            core_in.at[k],
            core_send.at[k],
            core_recv.at[k],
            p.at(p.z, p.y, 1 - p.core),
        )

    def y_copy(z):
        return remote(
            y_out.at[z], y_in.at[z], y_send.at[z], y_recv.at[z], p.at(p.z, 1 - p.y, p.core)
        )

    def up_copy(z):
        return remote(
            z_out.at[z], from_below.at[z], z_send.at[z], below_recv.at[z],
            p.at(p.z + 1, p.y, p.core),
        )

    def down_copy(z):
        return remote(
            z_out.at[z], from_above.at[z], z_send.at[z], above_recv.at[z],
            p.at(p.z - 1, p.y, p.core),
        )

    def compute(z):
        for side in sides:
            y = 1 - p.y if side == 1 else p.y
            k = z * p.wide + side
            core_out[k] = partial_of(z, y, 1 - p.core).astype(BF16)
            core_copy(z, side).start()
        for side in sides:
            y = 1 - p.y if side == 1 else p.y
            own[z * p.wide + side] = partial_of(z, y, p.core)

    def pair(z):
        for side in sides:
            k = z * p.wide + side
            core_copy(z, side).wait_recv()
            summed = own[k] + core_in[k].astype(F32)
            if side == 1:
                y_out[z] = summed.astype(BF16)
                y_copy(z).start()
            else:
                own[k] = summed

    def chain(z):
        k = z * p.wide
        if p.wide > 1:
            y_copy(z).wait_recv()
            own[k] = own[k] + y_in[z].astype(F32)

        @pl.when((z >= p.z) & (p.z > 0))
        def _():
            up_copy(z).wait_recv()
            own[k] = own[k] + from_below[z].astype(F32)

        @pl.when((z <= p.z) & (p.z < p.depth - 1))
        def _():
            down_copy(z).wait_recv()
            own[k] = own[k] + from_above[z].astype(F32)

        @pl.when(z != p.z)
        def _():
            z_out[z] = own[k].astype(BF16)

        @pl.when(z > p.z)
        def _():
            up_copy(z).start()

        @pl.when(z < p.z)
        def _():
            down_copy(z).start()

        @pl.when(z == p.z)
        def _():
            out[...] = own[k]

    in_order(compute)
    in_order(pair)
    in_order(chain)

    def drain(z):
        for side in sides:
            core_copy(z, side).wait_send()
        if p.wide > 1:
            y_copy(z).wait_send()

        @pl.when(z != p.z)
        def _():
            up_copy(z).wait_send()

    in_order(drain)


def back(n, left, basis_in):
    features, width = basis_in.shape
    depth, wide = grid_of(n)
    sems = pltpu.SemaphoreType.DMA
    piece = (OUT_ROWS, width)
    return pl.pallas_call(
        functools.partial(back_kernel, n),
        out_shape=jax.ShapeDtypeStruct(piece, F32),
        in_specs=[
            pl.BlockSpec(memory_space=pltpu.VMEM),
            pl.BlockSpec(memory_space=pl.ANY),
        ],
        out_specs=pl.BlockSpec(memory_space=pltpu.VMEM),
        scratch_shapes=[
            pltpu.VMEM((n, width, width), F32),
            pltpu.VMEM((depth * wide, *piece), F32),
            pltpu.VMEM((depth * wide, *piece), BF16),
            pltpu.VMEM((depth * wide, *piece), BF16),
            pltpu.VMEM((depth, *piece), BF16),
            pltpu.VMEM((depth, *piece), BF16),
            pltpu.VMEM((depth, *piece), BF16),
            pltpu.VMEM((depth, *piece), BF16),
            pltpu.VMEM((depth, *piece), BF16),
            sems((n,)),
            sems((depth * wide,)),
            sems((depth * wide,)),
            sems((depth,)),
            sems((depth,)),
            sems((depth,)),
            sems((depth,)),
            sems((depth,)),
        ],
        compiler_params=pltpu.CompilerParams(
            collective_id=1, has_side_effects=True, vmem_limit_bytes=VMEM_BYTES
        ),
        name="back_rotate",
    )(left, basis_in)


def per_device(n, acts, grads, lengths, basis_in, basis_out):
    rows = jnp.concatenate([acts.reshape(ROW_TILE, -1), grads.reshape(ROW_TILE, -1)], 0)
    rot_out, window, rot_in, damp = rotate_all(n, rows, lengths, basis_in, basis_out)
    corrections, left = correct(lengths, rot_out, window, rot_in, damp)
    precond = back(n, left, basis_in)
    return (corrections, precond)


def solution(mesh):
    in_specs = (
        P(("groups", "eigen"), None),
        P(("groups", "eigen"), None),
        P("groups"),
        P("groups", "eigen"),
        P("groups", "eigen"),
    )
    out_specs = (P("groups", "eigen"), P("groups", "eigen"))
    return jax.shard_map(
        functools.partial(per_device, mesh.shape["eigen"]),
        mesh=mesh,
        in_specs=in_specs,
        out_specs=out_specs,
        check_vma=False,
    )
```

time: 318 us -> 104 us (0.33)
  matrix products: 100 us -> 0 us
  Pallas kernels: 0 us -> 98.7 us
  blocking collectives: 98.4 us -> 0 us
  waiting for transfers between devices: 69.3 us -> 0 us
  other arithmetic: 24 us -> 0.64 us
  between operations: 22.2 us -> 0.65 us
    dot_general x5 -> x0, matrix products: 100 us -> none  [the longest x1 33.2 us: per_device(): jnp.dot(lax.all_gather(window, 'eigen', axis=1, tiled=True), scaled, prec...]
    pallas_call x0 -> x3, Pallas kernels: none -> 98.7 us  [the longest x1 52.3 us: rotate_all(): pl.pallas_call(functools.partial(rotate_kernel, n), out_shape=(jax.ShapeD...]
    reduce_scatter x1 -> x0, waiting for transfers between devices: 69.2 us -> none  [per_device(): lax.psum_scatter(jnp.dot(basis_in, left_part.T, precision=highest, prefer...]
    all_gather x3 -> x0, blocking collectives: 67.5 us -> none  [the longest x1 26.3 us: per_device(): lax.all_gather(grads, 'eigen', axis=0, tiled=True)]
    psum x1 -> x0, blocking collectives: 30.9 us -> none  [per_device(): total_all = lax.psum(jnp.sum(corrections), 'eigen')]
    reduce_sum x1 -> x0, other arithmetic: 13.5 us -> none  [per_device(): total_all = lax.psum(jnp.sum(corrections), 'eigen')]
    convert_element_type x4 -> x0, other arithmetic: 8.99 us -> none  [per_device(): ((where >= starts[seq_id]) & (where < ends[seq_id])).astype(jnp.bfloat16)]
  transfers between devices with their start and end apart: 2 -> 0, of which waited for: 1 -> 0; matrix products, arithmetic and copies ran while one was open for 22% -> 0% of each run, Pallas kernels for 0% -> 0%
where the time goes in v1:
time: 104 us; the launch traced here: 103 us
  Pallas kernels  98.7 us (95%)
  local copies, waits for them, and re-layouts  3.23 us (3%)
    pallas_call x1, Pallas kernels, rotate_all(): pl.pallas_call(functools.partial(rotate_kernel, n), out_shape=(jax.ShapeD...  52.3 us
    pallas_call x1, Pallas kernels, back(): pl.pallas_call(functools.partial(back_kernel, n), out_shape=jax.ShapeDtyp...  27.3 us
    pallas_call x1, Pallas kernels, correct(): pl.pallas_call(correct_kernel, grid=(n,), out_shape=(jax.ShapeDtypeStruct...  19.1 us

profile of v1, /device:TPU:0, one launch (start us, length us, event | category | flops | bytes accessed | tf_op | source)
XLA Modules:
  0.0 103.2 jit_solution(13985385190334970517)
XLA Ops:
  0.6 0.8 reshape.10
  1.4 0.8 reshape.11
  2.2 0.6 pad_maximum_fusion.rows_ref
  2.8 52.3 %rotate_and_gather.1 = (bf16[16,32,512]{2,1,0:T(8,128)(2,1)}, bf16[16,128,512]{2,1,0:T(8,128)(2,1)}, bf16[32,512]{1,0:T(8,128)(2,1)}, f32[8,128]{1,0:T(8,128)}) custom-call(bf16[32,1024]{1,0:T(8,128)(2,1)} %pad_maximum_fusion.rows_ref, s32[4]{0:T(128)} %lengths.3, f32[8192,512]{1,0:T(8,128)} %basis.1, f32[8192,512]{1,0:T(8,128)} %basis_out.1), custom_call_target="tpu_custom_call" | custom-call | tf_op jit(solution)/shard_map/rotate_and_gather/pallas_call | solution.py:347
  55.1 19.1 %corrections.1 = (f32[8192,512]{1,0:T(8,128)}, f32[128,512]{1,0:T(8,128)}) custom-call(s32[4]{0:T(128)} %lengths.3, bf16[16,32,512]{2,1,0:T(8,128)(2,1)} %get-tuple-element.8.rot_out, bf16[16,128,512]{2,1,0:T(8,128)(2,1)} %get-tuple-element.9.window, bf16[32,512]{1,0:T(8,128)(2,1)} %get-tuple-element.10.rot_in, f32[8,128]{1,0:T(8,128)} %get-tuple-element.11.damp), custom_call_target="tpu_custom_call" | custom-call | tf_op jit(solution)/shard_map/corrections/pallas_call | solution.py:432
  74.3 27.3 %back_rotate.1 = f32[128,512]{1,0:T(8,128)} custom-call(f32[128,512]{1,0:T(8,128)} %get-tuple-element.13.left_ref, f32[8192,512]{1,0:T(8,128)} %basis.1), custom_call_target="tpu_custom_call" | custom-call | tf_op jit(solution)/shard_map/back_rotate/pallas_call | solution.py:618
  101.5 1.7 %copy.8 = f32[128,512]{1,0:T(8,128)} copy(f32[128,512]{1,0:T(8,128)} %back_rotate.1) | data formatting | bytes 524288

commit v2 on v1

--- a/solution.py
+++ b/solution.py
@@ -11,6 +11,8 @@
 OUT_ROWS = 128
 CORES = 2
 ROW_TILE = 16
+BANDS = 4
+GROUP = 4
 damp_share = 0.1
 BF16 = jnp.bfloat16
 F32 = jnp.float32
@@ -71,31 +73,34 @@
         )
 
     def arrived(self, slot):
-        self.copy(slot, 0, self.p.me).wait_recv()
-
-    def up(self, slot, act):
-        p = self.p
-
-        @pl.when(p.z < p.depth - 1)
-        def _():
-            act(self.copy(slot, 0, p.at(p.z + 1, p.y, p.core)))
-
-    def down(self, slot, act):
-        p = self.p
-
-        @pl.when(p.z > 0)
-        def _():
-            act(self.copy(slot, 1, p.at(p.z - 1, p.y, p.core)))
+        self.copy(slot, 0, self.p.at(self.p.z, self.p.y, 1 - self.p.core)).wait_recv()
+
+    def along(self, act):
+        p = self.p
+        for h in range(p.depth - 1, 0, -1):
+            for there in (p.z + h, p.z - h):
+
+                @pl.when((there >= 0) & (there < p.depth))
+                def _():
+                    act(
+                        remote(
+                            self.slots.at[p.me],
+                            self.slots.at[p.me],
+                            self.send_sems.at[0, there],
+                            self.recv_sems.at[p.me],
+                            p.at(there, p.y, p.core),
+                        )
+                    )
 
     def across(self, slot, act):
         p = self.p
         if p.wide > 1:
-            act(self.copy(slot, 2, p.at(p.z, 1 - p.y, p.core)))
+            act(self.copy(slot, 1, p.at(p.z, 1 - p.y, p.core)))
         self.over(slot, act)
 
     def over(self, slot, act):
         p = self.p
-        act(self.copy(slot, 3, p.at(p.z, p.y, 1 - p.core)))
+        act(self.copy(slot, 2, p.at(p.z, p.y, 1 - p.core)))
 
     def beside(self, dz):
         p = self.p
@@ -107,8 +112,7 @@
     def round(self, h):
         p = self.p
         if h == 0:
-            self.up(p.me, start)
-            self.down(p.me, start)
+            self.along(start)
             self.across(p.me, start)
             return
 
@@ -116,14 +120,12 @@
         def _():
             slot = p.at(p.z - h, p.y, p.core)
             self.arrived(slot)
-            self.up(slot, start)
             self.across(slot, start)
 
         @pl.when(p.z + h < p.depth)
         def _():
             slot = p.at(p.z + h, p.y, p.core)
             self.arrived(slot)
-            self.down(slot, start)
             self.across(slot, start)
 
         self.beside_round(h - 1)
@@ -151,18 +153,9 @@
 
     def drain(self):
         p = self.p
+        self.along(wait_send)
         for z in range(p.depth):
-            slot = p.at(z, p.y, p.core)
-
-            @pl.when(z <= p.z)
-            def _():
-                self.up(slot, wait_send)
-
-            @pl.when(z >= p.z)
-            def _():
-                self.down(slot, wait_send)
-
-            self.across(slot, wait_send)
+            self.across(p.at(z, p.y, p.core), wait_send)
             if p.wide > 1:
                 self.over(p.at(z, 1 - p.y, p.core), wait_send)
 
@@ -192,7 +185,8 @@
 
 def rotate_kernel(
     n,
-    rows_ref,
+    acts_ref,
+    grads_ref,
     lengths,
     basis_in,
     basis_out,
@@ -201,7 +195,9 @@
     rot_in_ref,
     damp_ref,
     held,
+    rows,
     tokens,
+    lefts,
     window_f32,
     window,
     rot_out,
@@ -238,60 +234,66 @@
         for k in range(steps):
             load(which, k).start()
 
-    tokens[place.me] = rows_ref[...]
+    for base, source in ((0, acts_ref), (ROW_TILE, grads_ref)):
+        whole = source[...].astype(F32)
+        for r in range(ROW_TILE):
+            t, k = r // steps, r % steps
+            rows[base + r : base + r + 1, :] = whole[t : t + 1, k * chunk : (k + 1) * chunk]
+    tokens[place.me] = rows[...].astype(BF16)
     entry_barrier(place)
     token_gather = Gather(place, tokens, token_send, token_recv)
     window_gather = Gather(place, window, window_send, window_recv)
     rot_gather = Gather(place, rot_out, rot_send, rot_recv)
-    for h in range(place.depth):
+    token_gather.round(0)
+    first_rows.wait()
+    window[place.me] = window_f32[...].astype(BF16)
+    window_gather.along(start)
+    for h in range(1, place.depth):
         token_gather.round(h)
     token_gather.last()
-    first_rows.wait()
-    window[place.me] = window_f32[...].astype(BF16)
-    window_gather.round(0)
-
-    def rotate(which, low, high):
-        row = lax.broadcasted_iota(jnp.int32, (count, n * ROW_TILE), 0)
-        col = lax.broadcasted_iota(jnp.int32, (count, n * ROW_TILE), 1)
+    window_gather.across(place.me, start)
+
+    def arrange(which):
+        row = lax.broadcasted_iota(jnp.int32, (n * ROW_TILE, n * ROW_TILE), 0)
+        col = lax.broadcasted_iota(jnp.int32, (n * ROW_TILE, n * ROW_TILE), 1)
+        pick = (col == lax.rem(row, count) * steps + row // count).astype(F32).astype(BF16)
         here = pl.ds((1 - which) * ROW_TILE, ROW_TILE)
         flat = tokens[:, here, :].reshape(n * ROW_TILE, chunk)
-
-        def body(k, carry):
+        lefts[which] = jnp.dot(pick, flat, preferred_element_type=F32).astype(BF16)
+
+    def rotate(which, low, high):
+        for k in range(low, high):
             load(which, k).wait()
-            pick = (col == row * steps + k).astype(F32).astype(BF16)
-            left = jnp.dot(pick, flat, preferred_element_type=F32).astype(BF16)
+            left = lefts[which, k * count : (k + 1) * count, :]
             block = held[which, k]
             high_part = block.astype(BF16)
             low_part = (block - high_part.astype(F32)).astype(BF16)
             acc[...] += jnp.dot(left, high_part, preferred_element_type=F32) + jnp.dot(
                 left, low_part, preferred_element_type=F32
             )
-            return carry
-
-        lax.fori_loop(low, high, body, 0)
-
-    half = steps // 2
-    rounds = list(range(1, place.depth))
+
+    later = list(range(1, place.depth))
+    arrange(0)
     acc[...] = jnp.zeros_like(acc)
-    rotate(0, 0, half)
-    for h in rounds[:1]:
+    rotate(0, 0, steps // 4)
+    for h in later[:1]:
         window_gather.round(h)
-    rotate(0, half, steps)
+    rotate(0, steps // 4, steps * 5 // 8)
+    for h in later[1:2]:
+        window_gather.round(h)
+    rotate(0, steps * 5 // 8, steps)
     rot_out[place.me] = acc[...].astype(BF16)
     rot_gather.round(0)
-    for h in rounds[1:2]:
+    for h in later[2:]:
         window_gather.round(h)
+    arrange(1)
     acc[...] = jnp.zeros_like(acc)
-    rotate(1, 0, half)
-    for h in rounds[:1]:
+    rotate(1, 0, steps // 2)
+    for h in later:
         rot_gather.round(h)
-    for h in rounds[2:]:
-        window_gather.round(h)
-    rotate(1, half, steps)
+    rotate(1, steps // 2, steps)
     rot_in = acc[...].astype(BF16)
     rot_in_ref[...] = rot_in
-    for h in rounds[1:]:
-        rot_gather.round(h)
     rot_gather.last()
 
     contract = (((1,), (1,)), ((), ()))
@@ -338,11 +340,11 @@
     window_copy.wait()
 
 
-def rotate_all(n, rows, lengths, basis_in, basis_out):
+def rotate_all(n, acts, grads, lengths, basis_in, basis_out):
     features, width = basis_in.shape
-    chunk = rows.shape[1]
-    steps = features // chunk
-    count = n * ROW_TILE // steps
+    steps = ROW_TILE // acts.shape[0]
+    chunk = features // steps
+    count = n * acts.shape[0]
     sems = pltpu.SemaphoreType.DMA
     return pl.pallas_call(
         functools.partial(rotate_kernel, n),
@@ -353,6 +355,7 @@
             jax.ShapeDtypeStruct((8, 128), F32),
         ),
         in_specs=[
+            pl.BlockSpec(memory_space=pltpu.VMEM),
             pl.BlockSpec(memory_space=pltpu.VMEM),
             pl.BlockSpec(memory_space=pltpu.SMEM),
             pl.BlockSpec(memory_space=pl.ANY),
@@ -366,18 +369,20 @@
         ),
         scratch_shapes=[
             pltpu.VMEM((2, steps, chunk, width), F32),
+            pltpu.VMEM((2 * ROW_TILE, chunk), F32),
             pltpu.VMEM((n, 2 * ROW_TILE, chunk), BF16),
+            pltpu.VMEM((2, steps * count, chunk), BF16),
             pltpu.VMEM((OUT_ROWS, width), F32),
             pltpu.VMEM((n, OUT_ROWS, width), BF16),
             pltpu.VMEM((n, count, width), BF16),
             pltpu.VMEM((n, 8, 128), F32),
             pltpu.VMEM((count, width), F32),
             sems((2, steps)),
-            sems((4, n)),
+            sems((3, n)),
             sems((n,)),
-            sems((4, n)),
+            sems((3, n)),
             sems((n,)),
-            sems((4, n)),
+            sems((3, n)),
             sems((n,)),
             sems((n,)),
             sems((n,)),
@@ -387,7 +392,7 @@
             collective_id=0, has_side_effects=True, vmem_limit_bytes=VMEM_BYTES
         ),
         name="rotate_and_gather",
-    )(rows, lengths, basis_in, basis_out)
+    )(acts, grads, lengths, basis_in, basis_out)
 
 
 def correct_kernel(lengths, rot_out, window, rot_in, damp, corrections, left, masked):
@@ -404,8 +409,10 @@
             masked[:, s * width : (s + 1) * width] = jnp.where(which == s, half, 0.0).astype(BF16)
         left[...] = jnp.zeros_like(left)
 
-    columns = rot_out[0].astype(F32).T.astype(BF16)
-    tile = 64
+    columns = jnp.concatenate(
+        [rot_out[g].astype(F32).T.astype(BF16) for g in range(rot_out.shape[0])], 0
+    )
+    tile = 128
     damping = damp[0:1, 0:1]
     scaled = []
     for low in range(0, columns.shape[0], tile):
@@ -418,8 +425,14 @@
             squares = product * product if s == 0 else squares + product * product
             total = product if s == 0 else total + product
         corrections[low : low + tile, :] = squares
-        scaled.append((total / (squares + damping)).astype(BF16))
-    left[...] += jnp.dot(window[0], jnp.concatenate(scaled, 0), preferred_element_type=F32)
+        scaled.append((total * pl.reciprocal(squares + damping, approx=True)).astype(BF16))
+    per = len(scaled) // rot_out.shape[0]
+    for g in range(rot_out.shape[0]):
+        left[...] += jnp.dot(
+            window[g],
+            jnp.concatenate(scaled[g * per : (g + 1) * per], 0),
+            preferred_element_type=F32,
+        )
 
     @pl.when(block == pl.num_programs(0) - 1)
     def _():
@@ -431,20 +444,20 @@
     whole = lambda i: (0, 0)
     return pl.pallas_call(
         correct_kernel,
-        grid=(n,),
+        grid=(n // GROUP,),
         out_shape=(
             jax.ShapeDtypeStruct((n * width, width), F32),
             jax.ShapeDtypeStruct((OUT_ROWS, width), F32),
         ),
         in_specs=[
             pl.BlockSpec(memory_space=pltpu.SMEM),
-            pl.BlockSpec((1, count, width), lambda i: (i, 0, 0)),
-            pl.BlockSpec((1, OUT_ROWS, width), lambda i: (i, 0, 0)),
+            pl.BlockSpec((GROUP, count, width), lambda i: (i, 0, 0)),
+            pl.BlockSpec((GROUP, OUT_ROWS, width), lambda i: (i, 0, 0)),
             pl.BlockSpec((count, width), whole),
             pl.BlockSpec((8, 128), whole),
         ],
         out_specs=(
-            pl.BlockSpec((width, width), lambda i: (i, 0)),
+            pl.BlockSpec((GROUP * width, width), lambda i: (i, 0)),
             pl.BlockSpec((OUT_ROWS, width), whole),
         ),
         scratch_shapes=[pltpu.VMEM((count, SEQS * width), BF16)],
@@ -465,16 +478,14 @@
     y_out,
     y_in,
     z_out,
-    from_below,
-    from_above,
+    z_in,
     held_sems,
     core_send,
     core_recv,
     y_send,
     y_recv,
     z_send,
-    below_recv,
-    above_recv,
+    z_recv,
 ):
     place = Place(n)
     p = place
@@ -485,22 +496,24 @@
             basis.at[pl.ds(pl.multiple_of(d * width, width), width)], held.at[d], held_sems.at[d]
         )
 
-    def in_order(visit):
-        for h in range(p.depth - 1, 0, -1):
-            for there in (p.z + h, p.z - h):
-
-                @pl.when((there >= 0) & (there < p.depth))
-                def _():
-                    visit(there)
-
-        visit(p.z)
+    far, near = jnp.maximum(p.z, p.depth - 1 - p.z), jnp.minimum(p.z, p.depth - 1 - p.z)
+
+    def turn(i):
+        alone = jnp.where(p.z < p.depth - 1 - p.z, p.depth - 1 - i, i)
+        j = jnp.maximum(i - (far - near), 0)
+        reach = near - j // 2
+        paired = jnp.where(lax.rem(j, 2) == 0, p.z + reach, p.z - reach)
+        return jnp.where(i < far - near, alone, paired)
+
+    turns = [turn(i) for i in range(p.depth)]
 
     def load_all(z):
         for y in range(p.wide):
             for core in range(CORES):
                 load(p.at(z, y, core)).start()
 
-    in_order(load_all)
+    for z in turns:
+        load_all(z)
     left = left_ref[...].astype(BF16)
     entry_barrier(place)
 
@@ -523,28 +536,33 @@
             p.at(p.z, p.y, 1 - p.core),
         )
 
-    def y_copy(z):
+    def y_copy(z, b):
         return remote(
-            y_out.at[z], y_in.at[z], y_send.at[z], y_recv.at[z], p.at(p.z, 1 - p.y, p.core)
-        )
-
-    def up_copy(z):
+            y_out.at[z, b],
+            y_in.at[z, b],
+            y_send.at[z, b],
+            y_recv.at[z, b],
+            p.at(p.z, 1 - p.y, p.core),
+        )
+
+    def z_copy(source, z, b):
         return remote(
-            z_out.at[z], from_below.at[z], z_send.at[z], below_recv.at[z],
-            p.at(p.z + 1, p.y, p.core),
-        )
-
-    def down_copy(z):
-        return remote(
-            z_out.at[z], from_above.at[z], z_send.at[z], above_recv.at[z],
-            p.at(p.z - 1, p.y, p.core),
-        )
+            z_out.at[z, b],
+            z_in.at[source, b],
+            z_send.at[z, b],
+            z_recv.at[source, b],
+            p.at(z, p.y, p.core),
+        )
+
+    part = OUT_ROWS // BANDS
+
+    def band(b):
+        return pl.ds(b * part, part)
 
     def compute(z):
         for side in sides:
             y = 1 - p.y if side == 1 else p.y
-            k = z * p.wide + side
-            core_out[k] = partial_of(z, y, 1 - p.core).astype(BF16)
+            core_out[z * p.wide + side] = partial_of(z, y, 1 - p.core).astype(BF16)
             core_copy(z, side).start()
         for side in sides:
             y = 1 - p.y if side == 1 else p.y
@@ -554,60 +572,59 @@
         for side in sides:
             k = z * p.wide + side
             core_copy(z, side).wait_recv()
-            summed = own[k] + core_in[k].astype(F32)
-            if side == 1:
-                y_out[z] = summed.astype(BF16)
-                y_copy(z).start()
-            else:
-                own[k] = summed
+            for b in range(BANDS):
+                summed = own[k, band(b), :] + core_in[k, band(b), :].astype(F32)
+                if side == 1:
+                    y_out[z, b] = summed.astype(BF16)
+                    y_copy(z, b).start()
+                else:
+                    own[k, band(b), :] = summed
 
     def chain(z):
         k = z * p.wide
-        if p.wide > 1:
-            y_copy(z).wait_recv()
-            own[k] = own[k] + y_in[z].astype(F32)
-
-        @pl.when((z >= p.z) & (p.z > 0))
-        def _():
-            up_copy(z).wait_recv()
-            own[k] = own[k] + from_below[z].astype(F32)
-
-        @pl.when((z <= p.z) & (p.z < p.depth - 1))
-        def _():
-            down_copy(z).wait_recv()
-            own[k] = own[k] + from_above[z].astype(F32)
-
-        @pl.when(z != p.z)
-        def _():
-            z_out[z] = own[k].astype(BF16)
-
-        @pl.when(z > p.z)
-        def _():
-            up_copy(z).start()
-
-        @pl.when(z < p.z)
-        def _():
-            down_copy(z).start()
-
-        @pl.when(z == p.z)
-        def _():
-            out[...] = own[k]
-
-    in_order(compute)
-    in_order(pair)
-    in_order(chain)
-
-    def drain(z):
+        for b in range(BANDS):
+            rows = band(b)
+            if p.wide > 1:
+                y_copy(z, b).wait_recv()
+                own[k, rows, :] = own[k, rows, :] + y_in[z, b].astype(F32)
+
+            @pl.when(z != p.z)
+            def _():
+                z_out[z, b] = own[k, rows, :].astype(BF16)
+                z_copy(p.z, z, b).start()
+
+    def finish():
+        k = p.z * p.wide
+        for b in range(BANDS):
+            rows = band(b)
+            for z in range(p.depth):
+
+                @pl.when(z != p.z)
+                def _():
+                    z_copy(z, z, b).wait_recv()
+                    own[k, rows, :] = own[k, rows, :] + z_in[z, b].astype(F32)
+
+            out[rows, :] = own[k, rows, :]
+
+    for i in range(p.depth + 2):
+        if i < p.depth:
+            compute(turns[i])
+        if 1 <= i <= p.depth:
+            pair(turns[i - 1])
+        if i >= 2:
+            chain(turns[i - 2])
+    finish()
+
+    for z in range(p.depth):
         for side in sides:
             core_copy(z, side).wait_send()
-        if p.wide > 1:
-            y_copy(z).wait_send()
-
-        @pl.when(z != p.z)
-        def _():
-            up_copy(z).wait_send()
-
-    in_order(drain)
+        for b in range(BANDS):
+            if p.wide > 1:
+                y_copy(z, b).wait_send()
+
+            @pl.when(z != p.z)
+            def _():
+                z_copy(p.z, z, b).wait_send()
 
 
 def back(n, left, basis_in):
@@ -615,6 +632,7 @@
     depth, wide = grid_of(n)
     sems = pltpu.SemaphoreType.DMA
     piece = (OUT_ROWS, width)
+    bands = (depth, BANDS, OUT_ROWS // BANDS, width)
     return pl.pallas_call(
         functools.partial(back_kernel, n),
         out_shape=jax.ShapeDtypeStruct(piece, F32),
@@ -628,19 +646,17 @@
             pltpu.VMEM((depth * wide, *piece), F32),
             pltpu.VMEM((depth * wide, *piece), BF16),
             pltpu.VMEM((depth * wide, *piece), BF16),
-            pltpu.VMEM((depth, *piece), BF16),
-            pltpu.VMEM((depth, *piece), BF16),
-            pltpu.VMEM((depth, *piece), BF16),
-            pltpu.VMEM((depth, *piece), BF16),
-            pltpu.VMEM((depth, *piece), BF16),
+            pltpu.VMEM(bands, BF16),
+            pltpu.VMEM(bands, BF16),
+            pltpu.VMEM(bands, BF16),
+            pltpu.VMEM(bands, BF16),
             sems((n,)),
             sems((depth * wide,)),
             sems((depth * wide,)),
-            sems((depth,)),
-            sems((depth,)),
-            sems((depth,)),
-            sems((depth,)),
-            sems((depth,)),
+            sems((depth, BANDS)),
+            sems((depth, BANDS)),
+            sems((depth, BANDS)),
+            sems((depth, BANDS)),
         ],
         compiler_params=pltpu.CompilerParams(
             collective_id=1, has_side_effects=True, vmem_limit_bytes=VMEM_BYTES
@@ -650,8 +666,7 @@
 
 
 def per_device(n, acts, grads, lengths, basis_in, basis_out):
-    rows = jnp.concatenate([acts.reshape(ROW_TILE, -1), grads.reshape(ROW_TILE, -1)], 0)
-    rot_out, window, rot_in, damp = rotate_all(n, rows, lengths, basis_in, basis_out)
+    rot_out, window, rot_in, damp = rotate_all(n, acts, grads, lengths, basis_in, basis_out)
     corrections, left = correct(lengths, rot_out, window, rot_in, damp)
     precond = back(n, left, basis_in)
     return (corrections, precond)

time: 104 us -> 92.5 us (0.89)
  Pallas kernels: 98.7 us -> 89.9 us
  local copies, waits for them, and re-layouts: 3.23 us -> 1.67 us
    pallas_call x1, Pallas kernels: 27.3 us -> 22.1 us  [back(): pl.pallas_call(functools.partial(back_kernel, n), out_shape=jax.ShapeDtyp...]
    pallas_call x1, Pallas kernels: 19.1 us -> 15.4 us  [correct(): pl.pallas_call(correct_kernel, grid=(n // GROUP,), out_shape=(jax.ShapeDt...]
    reshape x2 -> x0, local copies, waits for them, and re-layouts: 1.56 us -> none  [the longest x1 0.78 us: per_device(): grads.reshape(ROW_TILE, -1)]
where the time goes in v2:
time: 92.5 us; the launch traced here: 92.2 us
  Pallas kernels  89.9 us (97%)
  local copies, waits for them, and re-layouts  1.67 us (2%)
    pallas_call x1, Pallas kernels, rotate_all(): pl.pallas_call(functools.partial(rotate_kernel, n), out_shape=(jax.ShapeD...  52.3 us
    pallas_call x1, Pallas kernels, back(): pl.pallas_call(functools.partial(back_kernel, n), out_shape=jax.ShapeDtyp...  22.1 us
    pallas_call x1, Pallas kernels, correct(): pl.pallas_call(correct_kernel, grid=(n // GROUP,), out_shape=(jax.ShapeDt...  15.4 us

profile of v2, /device:TPU:0, one launch (start us, length us, event | category | flops | bytes accessed | tf_op | source)
XLA Modules:
  0.0 92.2 jit_solution(18111076360075875024)
XLA Ops:
  0.6 52.3 %rotate_and_gather.1 = (bf16[16,32,512]{2,1,0:T(8,128)(2,1)}, bf16[16,128,512]{2,1,0:T(8,128)(2,1)}, bf16[32,512]{1,0:T(8,128)(2,1)}, f32[8,128]{1,0:T(8,128)}) custom-call(bf16[2,8192]{1,0:T(2,128)(2,1)} %acts_ref.1, bf16[2,8192]{1,0:T(2,128)(2,1)} %grads_ref.1, s32[4]{0:T(128)} %lengths.3, f32[8192,512]{1,0:T(8,128)} %basis.1, f32[8192,512]{1,0:T(8,128)} %basis_out.1), custom_call_target="tpu_custom_call" | custom-call | tf_op jit(solution)/shard_map/rotate_and_gather/pallas_call | solution.py:349
  53.0 15.4 %corrections.1 = (f32[8192,512]{1,0:T(8,128)}, f32[128,512]{1,0:T(8,128)}) custom-call(s32[4]{0:T(128)} %lengths.3, bf16[16,32,512]{2,1,0:T(8,128)(2,1)} %get-tuple-element.8.rot_out, bf16[16,128,512]{2,1,0:T(8,128)(2,1)} %get-tuple-element.9.window, bf16[32,512]{1,0:T(8,128)(2,1)} %get-tuple-element.10.rot_in, f32[8,128]{1,0:T(8,128)} %get-tuple-element.11.damp), custom_call_target="tpu_custom_call" | custom-call | tf_op jit(solution)/shard_map/corrections/pallas_call | solution.py:445
  68.4 22.1 %back_rotate.1 = f32[128,512]{1,0:T(8,128)} custom-call(f32[128,512]{1,0:T(8,128)} %get-tuple-element.13.left_ref, f32[8192,512]{1,0:T(8,128)} %basis.1), custom_call_target="tpu_custom_call" | custom-call | tf_op jit(solution)/shard_map/back_rotate/pallas_call | solution.py:636
  90.5 1.7 %copy.8 = f32[128,512]{1,0:T(8,128)} copy(f32[128,512]{1,0:T(8,128)} %back_rotate.1) | data formatting | bytes 524288
